TPU v7x, 32 devices: a whole 2x2x4 slice. The times are simulated.
32 devices in a mesh: chain: 4 (over z), param: 8 (over y, x, core).
Axes of the slice: x: 2, y: 2, z: 4, core: 2. Of those that a mesh axis runs over, the one named last changes fastest.
Arguments:
- spins: int32 [128, 256, 4], P(('chain', 'param')), may hold values from 0 to 1
- local_energy: float32 [128], replicated, may hold values from -24 to 24
- embed_weight: float32 [4, 256], replicated, may hold values from -3 to 3
- position: bfloat16 [256, 256], replicated, may hold values from -6 to 6
- value_weight: bfloat16 [256, 256], replicated, may hold values from -0.375 to 0.375
- mixing: bfloat16 [8, 256, 256], replicated, may hold values from -0.375 to 0.375
- out_weight: bfloat16 [256, 256], replicated, may hold values from -0.375 to 0.375
- up_weight: bfloat16 [256, 1024], replicated, may hold values from -0.375 to 0.375
- down_weight: bfloat16 [1024, 256], replicated, may hold values from -0.1875 to 0.1875
- readout: float32 [256], replicated, may hold values from -6 to 6
Outputs:
- up_update: float32 [256, 1024], P('chain', 'param')
- down_update: float32 [1024, 256], P('param', 'chain')
- sample_weights: float32 [128], replicated
All inputs are finite; a program needn't handle non-finite values.
Results may differ from a plain program's by a relative error of at most 0.018.
Values may be sent and summed in bfloat16 or wider, within the bound.
A program may use at most 128 MiB of HBM per device.

v0:
```python
import math
import jax
import jax.numpy as jnp
from jax import lax
from jax.sharding import PartitionSpec as P

damping = 0.05


def layer_norm(hidden_state):
    average = jnp.mean(hidden_state, axis=-1, keepdims=True)
    centred = hidden_state - average
    spread = jnp.mean(centred * centred, axis=-1, keepdims=True)
    return centred * lax.rsqrt(spread + 1e-05)


def project(operand, weights):
    return lax.dot_general(
        operand,
        weights,
        (((operand.ndim - 1,), (0,)), ((), ())),
        preferred_element_type=jnp.float32,
    )


def center_rows(jacobian, total):
    jac_wide = jacobian.astype(jnp.float32)
    return (jac_wide - jnp.mean(jac_wide, axis=0)) / math.sqrt(total)


def gram_of(centred, total):
    flat = centred.reshape(total, -1)
    return lax.dot_general(
        flat,
        flat,
        (((1,), (1,)), ((), ())),
        precision=lax.Precision.HIGHEST,
        preferred_element_type=jnp.float32,
    )


def solve_weights(gram, local_energy, total):
    scale = jnp.trace(gram) / total
    system = gram + damping * scale * jnp.eye(total, dtype=jnp.float32)
    lower = jnp.linalg.cholesky(system)
    energy = (local_energy - jnp.mean(local_energy)) / math.sqrt(total)
    column = energy[:, None]
    middle = lax.linalg.triangular_solve(lower, column, left_side=True, lower=True)
    answer = lax.linalg.triangular_solve(
        lower, middle, left_side=True, lower=True, transpose_a=True
    )
    return scale * answer[:, 0]


def body(
    spins,
    local_energy,
    embed_weight,
    position,
    value_weight,
    mixing,
    out_weight,
    up_weight,
    down_weight,
    readout,
):
    samples = spins.shape[0]
    patch_rows = spins.shape[1]
    total = local_energy.shape[0]
    head_count = mixing.shape[0]
    model_width = value_weight.shape[0]
    spin_values = (2 * spins - 1).astype(jnp.float32)
    embedded = jnp.sum(spin_values[..., None] * embed_weight, axis=2) + position.astype(jnp.float32)
    normed = layer_norm(embedded).astype(jnp.bfloat16)
    values = project(normed, value_weight).astype(jnp.bfloat16)
    split_values = values.reshape(samples, patch_rows, head_count, model_width // head_count)
    mixture = jnp.einsum("htu,suhe->sthe", mixing, split_values, preferred_element_type=jnp.float32)
    mixture = mixture.astype(jnp.bfloat16).reshape(samples, patch_rows, model_width)
    residual = embedded + project(mixture, out_weight)
    features = layer_norm(residual).astype(jnp.bfloat16)
    preact = project(features, up_weight)
    hidden = jax.nn.gelu(preact).astype(jnp.bfloat16)
    output = residual + project(hidden, down_weight)
    cotangent = (readout * jnp.tanh(output)).astype(jnp.bfloat16)
    backward = lax.dot_general(
        cotangent, down_weight, (((2,), (1,)), ((), ())), preferred_element_type=jnp.float32
    )
    preact_grad = jax.vjp(jax.nn.gelu, preact)[1](backward)[0].astype(jnp.bfloat16)
    up_block = jnp.einsum("sti,stj->sij", features, preact_grad, preferred_element_type=jnp.float32)
    down_block = jnp.einsum("std,stj->sdj", cotangent, hidden, preferred_element_type=jnp.float32)
    jacobian = jnp.stack([up_block, down_block], axis=1).astype(jnp.bfloat16)
    grouped = lax.all_to_all(jacobian, "param", split_axis=3, concat_axis=0, tiled=True)
    chosen_raw = lax.all_to_all(grouped, "chain", split_axis=2, concat_axis=0, tiled=True)
    centred = center_rows(chosen_raw, total)
    gram = lax.psum(gram_of(centred, total), ("chain", "param"))
    sample_weights = solve_weights(gram, local_energy, total)
    update = -lax.dot_general(
        sample_weights,
        centred,
        (((0,), (0,)), ((), ())),
        precision=lax.Precision.HIGHEST,
        preferred_element_type=jnp.float32,
    )
    return (update[0], update[1].T, sample_weights)


def solution(mesh):
    in_specs = (P(("chain", "param"), None, None), P(), P(), P(), P(), P(), P(), P(), P(), P())
    out_specs = (P("chain", "param"), P("param", "chain"), P())
    return jax.shard_map(body, mesh=mesh, in_specs=in_specs, out_specs=out_specs, check_vma=False)
```

profile of v0, /device:TPU:1, one launch (start us, length us, event | category | flops | bytes accessed | tf_op | source)
XLA Modules:
  0.0 412.8 jit_solution(4878717197872433788)
XLA Ops:
  7.2 0.8 add_convert_fusion
  8.1 1.5 multiply_reduce_fusion
  9.9 1.0 copy.90
  12.7 0.8 fusion.26
  13.5 1.9 copy-done.3
  15.4 2.5 fusion.16
  17.9 6.1 %convert_bitcast_fusion.2 = bf16[4,1,256,1024]{3,2,0,1:T(8,128)(2,1)S(1)} fusion(f32[4,256,1024]{2,1,0:T(8,128)} %copy-done.3, bf16[4,256,256]{1,2,0:T(8,128)(2,1)} %fusion.16, bf16[1024,256]{1,0:T(8,128)(2,1)} %param.18, f32[4,256,256]{1,2,0:T(8,128)S(1)} %get-tuple-element.6, f32[4,256]{1,0:T(4,128)S(1)} %add_rsqrt_fusion, ...), kind=kOutput, calls=%fused_computation.21 | convolution fusion | flops 1096548352 | bytes 8396800 | tf_op jit(solution)/shard_map/sti,stj->sij/dot_general | solution.py:89
  24.0 4.1 convert_bitcast_fusion.1
  28.1 2.3 pad_maximum_fusion
  30.4 7.8 %copy.101 = bf16[4,2,256,1024]{2,0,1,3:T(4,128)(2,1)} copy(bf16[4,2,256,1024]{3,2,0,1:T(8,128)(2,1)} %pad_maximum_fusion) | data formatting | bytes 8388608 | tf_op jit(solution)/shard_map/stack | solution.py:91
  38.2 53.2 %all_to_all.27 = bf16[4,2,256,1024]{2,0,1,3:T(4,128)(2,1)S(1)} all-to-all(bf16[4,2,256,1024]{2,0,1,3:T(4,128)(2,1)} %copy.101), channel_id=1, replica_groups=mesh['chain'=4,'param'=8] {'param'}, dimensions={3} | all-to-all | bytes 8388608 | tf_op jit(solution)/shard_map/all_to_all | solution.py:92
  91.4 2.8 copy.102
  94.2 6.5 %copy.103 = bf16[8,4,2,256,128]{4,3,2,1,0:T(8,128)(2,1)} copy(bf16[8,4,2,256,128]{3,4,0,2,1:T(8,128)(2,1)} %bitcast.90) | data formatting | bytes 8388608 | tf_op jit(solution)/shard_map/all_to_all | solution.py:92
  100.6 6.5 %copy.104 = bf16[32,2,256,128]{3,1,0,2:T(2,128)(2,1)S(1)} copy(bf16[32,2,256,128]{3,2,1,0:T(8,128)(2,1)} %bitcast.91) | data formatting | bytes 8388608 | tf_op jit(solution)/shard_map/all_to_all | solution.py:92
  107.2 96.8 %all_to_all.28 = bf16[32,2,256,128]{3,1,0,2:T(2,128)(2,1)S(1)} all-to-all(bf16[32,2,256,128]{3,1,0,2:T(2,128)(2,1)S(1)} %copy.104), channel_id=1, replica_groups=mesh['chain'=4,'param'=8] {'chain'}, dimensions={2} | all-to-all | bytes 8388608 | tf_op jit(solution)/shard_map/all_to_all | solution.py:93
  203.9 4.9 %copy.105 = bf16[32,2,256,128]{3,2,1,0:T(8,128)(2,1)S(1)} copy(bf16[32,2,256,128]{3,1,0,2:T(2,128)(2,1)S(1)} %all_to_all.28) | data formatting | bytes 8388608 | tf_op jit(solution)/shard_map/all_to_all | solution.py:93
  208.8 0.8 fusion.1
  209.6 5.4 %fusion.2 = f32[4,32,2,64,128]{4,3,0,2,1:T(8,128)S(1)} fusion(f32[2,64,128]{2,1,0:T(8,128)S(1)} %broadcast_multiply_fusion, bf16[32,2,256,128]{3,1,0,2:T(2,128)(2,1)S(1)} %all_to_all.28), kind=kLoop, calls=%fused_computation.3 | loop fusion | flops 6291456 | bytes 12648448 | tf_op jit(solution)/shard_map/div | solution.py:28
  215.0 10.4 %copy.106 = f32[4,32,2,64,128]{4,3,2,1,0:T(8,128)S(1)} copy(f32[4,32,2,64,128]{4,3,0,2,1:T(8,128)S(1)} %fusion.2) | data formatting | bytes 16777216 | tf_op jit(solution)/shard_map/div | solution.py:28
  225.4 3.2 copy-done.2
  228.7 17.1 %fusion.18 = f32[128,128]{1,0:T(8,128)} fusion(f32[128,2,64,128]{3,2,1,0:T(8,128)S(1)} %bitcast.88), kind=kOutput, calls=%fused_computation.30 | convolution fusion | flops 3221225472 | bytes 8454144 | tf_op jit(solution)/shard_map/dot_general | solution.py:33
  245.8 0.6 reduce_sum.80
  247.1 117.5 %all-reduce.2.cloned.1.call-done = f32[128,128]{1,0:T(8,128)} async-done(((f32[128,128]{1,0:T(8,128)}), f32[128,128]{1,0:T(8,128)}) %all-reduce.2.cloned.1.call-update) | async-done | bytes 65552 | tf_op jit(solution)/shard_map/psum | solution.py:95
  364.5 1.5 select_reduce_fusion.1
  367.3 0.9 select_add_fusion
  368.2 0.9 fusion.37
  369.1 11.7 %cholesky.13 = f32[128,128]{1,0:T(8,128)S(1)} custom-call(f32[128,128]{1,0:T(8,128)S(1)} %fusion.37), custom_call_target="Cholesky" | custom-call | tf_op jit(solution)/shard_map/jit(cholesky)/cholesky | solution.py:45
  380.8 0.6 compare_reduce_fusion
  381.5 0.7 fusion.34
  382.1 9.8 %custom-call.8 = f32[1,128,128]{1,2,0:T(8,128)S(1)} custom-call(f32[1,128,128]{2,1,0:T(8,128)S(1)} %fusion.34), custom_call_target="InvertDiagBlocksLowerTriangular" | custom-call | tf_op jit(solution)/shard_map/triangular_solve | solution.py:49
  392.3 12.5 %fusion.3 = f32[1,2,64,128]{3,0,2,1:T(1,128)S(1)} fusion(f32[128,2,64,128]{3,2,1,0:T(8,128)} %bitcast.89, f32[128]{0:T(128)S(1)} %fusion.21), kind=kOutput, calls=%fused_computation.4 | convolution fusion | flops 25165824 | bytes 8454656 | tf_op jit(solution)/shard_map/dot_general | solution.py:97
  404.9 0.6 slice_bitcast_fusion
  (40 shorter events, 2.5 us)
Async XLA Ops:
  7.2 4.4 %copy-start = (bf16[8,256,256]{2,1,0:T(8,128)(2,1)S(1)}, bf16[8,256,256]{2,1,0:T(8,128)(2,1)}, u32[]{:S(2)}) copy-start(bf16[8,256,256]{2,1,0:T(8,128)(2,1)} %param.15) | copy-start | bytes 3145732
  7.2 4.0 copy-start.6
  7.2 357.3 %all-reduce.2.cloned.1.call-start = ((), (), s32[]{:S(2)}) async-start(), calls=%async_computation.2 | async-start | bytes 131072 | tf_op jit(solution)/shard_map/psum | solution.py:95
  9.9 2.3 copy-start.5
  11.2 1.5 copy-start.4
  12.1 3.2 copy-start.9
  12.2 3.2 copy-start.10
  13.4 1.9 copy-start.3
  225.4 3.2 copy-start.2
  228.7 17.1 %copy-start.8 = (f32[128]{0:T(128)S(1)}, f32[128]{0:T(128)}, u32[]{:S(2)}) copy-start(f32[128]{0:T(128)} %param.11) | copy-start | bytes 1540
  392.1 13.4 %copy-start.1 = (bf16[8,256,256]{2,1,0:T(8,128)(2,1)S(1)}, bf16[8,256,256]{2,1,0:T(8,128)(2,1)}, u32[]{:S(2)}) copy-start(bf16[8,256,256]{2,1,0:T(8,128)(2,1)} %param.15) | copy-start | bytes 3145732
  392.3 12.5 %copy-start.7 = (f32[128]{0:T(128)}, f32[128]{0:T(128)S(1)}, u32[]{:S(2)}) copy-start(f32[128]{0:T(128)S(1)} %fusion.21) | copy-start | bytes 1540
Sparse Core Ops, SparseCore 0:
  245.9 118.5 all-reduce.1
where the time goes:
time: 421 us; the launch traced here: 413 us
  blocking collectives  150 us (36%)
  waiting for transfers between devices  117 us (28%)
  local copies, waits for them, and re-layouts  46.1 us (11%)
  matrix products  44.6 us (11%)
  other arithmetic  37.8 us (9%)
  between operations  16.7 us (4%)
    psum x1, waiting for transfers between devices, body(): gram = lax.psum(gram_of(centred, total), ('chain', 'param'))  117 us
    all_to_all x1, blocking collectives, body(): lax.all_to_all(grouped, 'chain', split_axis=2, concat_axis=0, tiled=True)  96.8 us
    all_to_all x1, blocking collectives, body(): lax.all_to_all(jacobian, 'param', split_axis=3, concat_axis=0, tiled=True)  53.2 us
    dot_general x1, matrix products, gram_of(): lax.dot_general(flat, flat, (((1,), (1,)), ((), ())), precision=lax.Preci...  17.1 us
    all_to_all x3, local copies, waits for them, and re-layouts, body(): lax.all_to_all(jacobian, 'param', split_axis=3, concat_axis=0, tiled=True)  15.7 us
    dot_general x1, matrix products, body(): lax.dot_general(sample_weights, centred, (((0,), (0,)), ((), ())), precis...  12.5 us
    another operation x3, other arithmetic, solve_weights(): lower = jnp.linalg.cholesky(system)  12.4 us
    another operation x2, other arithmetic, solve_weights(): lax.linalg.triangular_solve(lower, middle, left_side=True, lower=True, tr...  10.5 us
  transfers between devices with their start and end apart: 1, of which 1 were waited for; matrix products, arithmetic and copies ran while one was open for 0% of the time, Pallas kernels for 0%

commit v1 on v0

--- a/solution.py
+++ b/solution.py
@@ -89,7 +89,28 @@
     up_block = jnp.einsum("sti,stj->sij", features, preact_grad, preferred_element_type=jnp.float32)
     down_block = jnp.einsum("std,stj->sdj", cotangent, hidden, preferred_element_type=jnp.float32)
     jacobian = jnp.stack([up_block, down_block], axis=1).astype(jnp.bfloat16)
-    grouped = lax.all_to_all(jacobian, "param", split_axis=3, concat_axis=0, tiled=True)
+
+    def trace_strings_on(m, mesh_dim):
+        formed = lax.axis_index(mesh_dim)
+        carry_out = lax.axis_size(mesh_dim)
+        extra, x_next = (carry_out, formed)
+        f_now = list(m.shape)
+        row_out = m.shape[3] // extra
+        f_now[3] = row_out
+        h_now = f_now[0]
+        f_now[0] = h_now * extra
+        after = jnp.zeros(f_now, m.dtype)
+        for dd in range(extra):
+            base_arr = lax.dynamic_slice_in_dim(m, (x_next ^ dd) * row_out, row_out, axis=3)
+            if dd:
+                rows = []
+                for num in range(extra):
+                    rows.append((num, num ^ dd))
+                base_arr = lax.ppermute(base_arr, axis_name=mesh_dim, perm=rows)
+            after = lax.dynamic_update_slice_in_dim(after, base_arr, (x_next ^ dd) * h_now, axis=0)
+        return after
+
+    grouped = trace_strings_on(jacobian, "param")
     chosen_raw = lax.all_to_all(grouped, "chain", split_axis=2, concat_axis=0, tiled=True)
     centred = center_rows(chosen_raw, total)
     gram = lax.psum(gram_of(centred, total), ("chain", "param"))

time: 421 us -> 389 us (0.924)
  blocking collectives: 150 us -> 97.6 us
  waiting for transfers between devices: 117 us -> 142 us
  local copies, waits for them, and re-layouts: 46.1 us -> 33.8 us
  starting transfers between devices: 0.04 us -> 7.49 us
    all_to_all x1 -> x0, blocking collectives: 53.2 us -> none  [body(): lax.all_to_all(jacobian, 'param', split_axis=3, concat_axis=0, tiled=True)]
    ppermute x0 -> x7, waiting for transfers between devices: none -> 23.5 us  [trace_strings_on(): base_arr = lax.ppermute(base_arr, axis_name=mesh_dim, perm=rows)]
    all_to_all x3 -> x0, local copies, waits for them, and re-layouts: 15.7 us -> none  [body(): lax.all_to_all(jacobian, 'param', split_axis=3, concat_axis=0, tiled=True)]
    dynamic_update_slice x0 -> x8, local copies, waits for them, and re-layouts: none -> 15.3 us  [trace_strings_on(): lax.dynamic_update_slice_in_dim(after, base_arr, (x_next ^ dd) * h_now, a...]
    div x1, local copies, waits for them, and re-layouts: 10.4 us -> 1.81 us  [center_rows(): return (jac_wide - jnp.mean(jac_wide, axis=0)) / math.sqrt(total)]
    another operation x1 -> x0, local copies, waits for them, and re-layouts: 7.85 us -> none  [body(): jacobian = jnp.stack([up_block, down_block], axis=1).astype(jnp.bfloat16)]
    ppermute x0 -> x7, starting transfers between devices: none -> 7.45 us  [trace_strings_on(): base_arr = lax.ppermute(base_arr, axis_name=mesh_dim, perm=rows)]
    broadcast_in_dim x0 -> x1, local copies, waits for them, and re-layouts: none -> 6.17 us  [trace_strings_on(): after = jnp.zeros(f_now, m.dtype)]
  transfers between devices with their start and end apart: 1 -> 8, of which waited for: 1 -> 3; matrix products, arithmetic and copies ran while one was open for 0% -> 6% of each run, Pallas kernels for 0% -> 0%
where the time goes in v1:
time: 389 us; the launch traced here: 382 us
  waiting for transfers between devices  142 us (37%)
  blocking collectives  97.6 us (25%)
  matrix products  43.4 us (11%)
  other arithmetic  41.6 us (11%)
  local copies, waits for them, and re-layouts  33.8 us (9%)
  between operations  16.8 us (4%)
  starting transfers between devices  7.49 us (2%)
    psum x1, waiting for transfers between devices, body(): gram = lax.psum(gram_of(centred, total), ('chain', 'param'))  118 us
    all_to_all x1, blocking collectives, body(): lax.all_to_all(grouped, 'chain', split_axis=2, concat_axis=0, tiled=True)  97.6 us
    ppermute x7, waiting for transfers between devices, trace_strings_on(): base_arr = lax.ppermute(base_arr, axis_name=mesh_dim, perm=rows)  23.5 us
    dot_general x1, matrix products, gram_of(): lax.dot_general(flat, flat, (((1,), (1,)), ((), ())), precision=lax.Preci...  17.1 us
    dynamic_update_slice x8, local copies, waits for them, and re-layouts, trace_strings_on(): lax.dynamic_update_slice_in_dim(after, base_arr, (x_next ^ dd) * h_now, a...  15.3 us
    dot_general x1, matrix products, body(): lax.dot_general(sample_weights, centred, (((0,), (0,)), ((), ())), precis...  12.5 us
    another operation x3, other arithmetic, solve_weights(): lower = jnp.linalg.cholesky(system)  12.4 us
    another operation x2, other arithmetic, solve_weights(): lax.linalg.triangular_solve(lower, middle, left_side=True, lower=True, tr...  10.5 us
  transfers between devices with their start and end apart: 8, of which 3 were waited for; matrix products, arithmetic and copies ran while one was open for 6% of the time, Pallas kernels for 0%

profile of v1, /device:TPU:1, one launch (start us, length us, event | category | flops | bytes accessed | tf_op | source)
XLA Modules:
  0.0 382.2 jit_solution(12246269645339529753)
XLA Ops:
  8.1 1.5 multiply_reduce_fusion
  9.9 1.0 copy.90
  13.5 1.7 fusion.16
  15.4 3.0 convert_bitcast_fusion.1
  18.5 6.7 %convert_bitcast_fusion.2 = bf16[4,1,256,1024]{3,2,0,1:T(8,128)(2,1)} fusion(f32[4,256,1024]{2,1,0:T(8,128)} %copy-done.3, bf16[4,256,256]{1,2,0:T(8,128)(2,1)S(1)} %fusion.16, bf16[1024,256]{1,0:T(8,128)(2,1)S(1)} %copy-done.13, f32[4,256,256]{1,2,0:T(8,128)S(1)} %get-tuple-element.14, f32[4,256]{1,0:T(4,128)S(1)} %add_rsqrt_fusion, ...), kind=kOutput, calls=%fused_computation.36 | convolution fusion | flops 1096548352 | bytes 8396800 | tf_op jit(solution)/shard_map/sti,stj->sij/dot_general | solution.py:89
  25.3 3.8 fusion.23
  29.1 2.7 collective-permute-start.1
  31.9 1.7 collective-permute-start.3
  33.5 2.2 fusion.30
  36.1 6.2 %broadcast_in_dim.6 = bf16[32,2,256,128]{3,1,0,2:T(2,128)(2,1)} broadcast(bf16[]{:T(256)} %constant.88.clone.1), dimensions={} | broadcast | bytes 4194306 | tf_op jit(solution)/shard_map/broadcast_in_dim | solution.py:102
  42.3 1.4 copy_dynamic-update-slice_fusion.7
  43.7 2.4 collective-permute-start.5
  46.1 2.4 copy_dynamic-update-slice_fusion.6
  48.8 2.4 copy_dynamic-update-slice_fusion.5
  51.2 4.7 %collective-permute-done.2 = bf16[4,2,256,128]{3,2,0,1:T(8,128)(2,1)} collective-permute-done((bf16[4,2,256,128]{3,2,0,1:T(8,128)(2,1)}, bf16[4,2,256,128]{3,2,0,1:T(8,128)(2,1)}, u32[]{:S(2)}, u32[]{:S(2)}) %collective-permute-start.2) | collective-permute-done | bytes 524320 | tf_op jit(solution)/shard_map/ppermute | solution.py:109
  56.0 2.4 copy_dynamic-update-slice_fusion.4
  58.4 2.4 copy_dynamic-update-slice_fusion.3
  60.9 18.8 %collective-permute-done.4 = bf16[4,2,256,128]{3,2,0,1:T(8,128)(2,1)S(1)} collective-permute-done((bf16[4,2,256,128]{3,2,0,1:T(8,128)(2,1)}, bf16[4,2,256,128]{3,2,0,1:T(8,128)(2,1)S(1)}, u32[]{:S(2)}, u32[]{:S(2)}) %collective-permute-start.4) | collective-permute-done | bytes 524320 | tf_op jit(solution)/shard_map/ppermute | solution.py:109
  79.6 1.4 copy_dynamic-update-slice_fusion.2
  81.0 1.4 copy_dynamic-update-slice_fusion.1
  82.4 1.4 copy_dynamic-update-slice_fusion
  83.8 97.6 %all_to_all.4 = bf16[32,2,256,128]{3,1,0,2:T(2,128)(2,1)S(1)} all-to-all(bf16[32,2,256,128]{3,1,0,2:T(2,128)(2,1)} %copy_dynamic-update-slice_fusion), channel_id=1, replica_groups=mesh['chain'=4,'param'=8] {'chain'}, dimensions={2} | all-to-all | bytes 8388608 | tf_op jit(solution)/shard_map/all_to_all | solution.py:114
  181.4 4.9 %copy.109 = bf16[32,2,256,128]{3,2,1,0:T(8,128)(2,1)S(1)} copy(bf16[32,2,256,128]{3,1,0,2:T(2,128)(2,1)S(1)} %all_to_all.4) | data formatting | bytes 8388608 | tf_op jit(solution)/shard_map/all_to_all | solution.py:114
  187.1 5.4 %fusion.2 = f32[4,32,2,64,128]{4,3,0,2,1:T(8,128)S(1)} fusion(f32[2,64,128]{2,1,0:T(8,128)S(1)} %broadcast_multiply_fusion, bf16[32,2,256,128]{3,1,0,2:T(2,128)(2,1)S(1)} %all_to_all.4), kind=kLoop, calls=%fused_computation.3 | loop fusion | flops 6291456 | bytes 12648448 | tf_op jit(solution)/shard_map/div | solution.py:28
  192.5 1.8 copy.110
  194.3 3.2 copy-done.1
  197.5 17.1 %fusion.18 = f32[128,128]{1,0:T(8,128)} fusion(f32[128,2,64,128]{3,2,1,0:T(8,128)S(1)} %bitcast.84), kind=kOutput, calls=%fused_computation.45 | convolution fusion | flops 3221225472 | bytes 8454144 | tf_op jit(solution)/shard_map/dot_general | solution.py:33
  215.9 118.0 %all-reduce.2.cloned.1.call-done = f32[128,128]{1,0:T(8,128)} async-done(((f32[128,128]{1,0:T(8,128)}), f32[128,128]{1,0:T(8,128)}) %all-reduce.2.cloned.1.call-update) | async-done | bytes 65552 | tf_op jit(solution)/shard_map/psum | solution.py:116
  333.9 1.5 select_reduce_fusion.1
  338.5 11.7 %cholesky.13 = f32[128,128]{1,0:T(8,128)S(1)} custom-call(f32[128,128]{1,0:T(8,128)S(1)} %fusion.45), custom_call_target="Cholesky" | custom-call | tf_op jit(solution)/shard_map/jit(cholesky)/cholesky | solution.py:45
  351.6 9.8 %custom-call.8 = f32[1,128,128]{1,2,0:T(8,128)S(1)} custom-call(f32[1,128,128]{2,1,0:T(8,128)S(1)} %fusion.42), custom_call_target="InvertDiagBlocksLowerTriangular" | custom-call | tf_op jit(solution)/shard_map/triangular_solve | solution.py:49
  361.7 12.5 %fusion.3 = f32[1,2,64,128]{3,0,2,1:T(1,128)S(1)} fusion(f32[128,2,64,128]{3,2,1,0:T(8,128)} %bitcast.85, f32[128]{0:T(128)S(1)} %fusion.21), kind=kOutput, calls=%fused_computation.20 | convolution fusion | flops 25165824 | bytes 8454656 | tf_op jit(solution)/shard_map/dot_general | solution.py:118
  (67 shorter events, 10.2 us)
Async XLA Ops:
  7.2 4.4 %copy-start = (bf16[8,256,256]{2,1,0:T(8,128)(2,1)S(1)}, bf16[8,256,256]{2,1,0:T(8,128)(2,1)}, u32[]{:S(2)}) copy-start(bf16[8,256,256]{2,1,0:T(8,128)(2,1)} %param.15) | copy-start | bytes 3145732
  7.2 4.0 %copy-start.9 = (bf16[256,256]{1,0:T(8,128)(2,1)S(1)}, bf16[256,256]{1,0:T(8,128)(2,1)}, u32[]{:S(2)}) copy-start(bf16[256,256]{1,0:T(8,128)(2,1)} %param.14) | copy-start | bytes 393220
  7.2 326.7 %all-reduce.2.cloned.1.call-start = ((), (), s32[]{:S(2)}) async-start(), calls=%async_computation.1 | async-start | bytes 131072 | tf_op jit(solution)/shard_map/psum | solution.py:116
  9.9 2.3 copy-start.8
  11.2 1.4 copy-start.6
  12.1 1.3 copy-start.12
  12.1 1.3 copy-start.14
  13.5 2.0 copy-start.3
  15.4 3.0 copy-start.13
  25.2 8.3 %copy-start.2 = (bf16[4,1,256,1024]{3,2,0,1:T(8,128)(2,1)S(1)}, bf16[4,1,256,1024]{3,2,0,1:T(8,128)(2,1)}, u32[]{:S(2)}) copy-start(bf16[4,1,256,1024]{3,2,0,1:T(8,128)(2,1)} %convert_bitcast_fusion.1) | copy-start | bytes 6291460
  29.1 14.7 %collective-permute-start = (bf16[4,2,256,128]{3,2,0,1:T(8,128)(2,1)}, bf16[4,2,256,128]{3,2,0,1:T(8,128)(2,1)}, u32[]{:S(2)}, u32[]{:S(2)}) collective-permute-start(bf16[4,2,256,128]{3,2,0,1:T(8,128)(2,1)} %get-tuple-element.5), channel_id=1, source_target_pairs={{0,1},{1,0},{2,3},{3,2},{4,5},{5,4},{6,7},{7,6},{8,9},{9,8},{10,11... | collective-permute-start | bytes 1572872 | tf_op jit(solution)/shard_map/ppermute | solution.py:109
  29.1 19.4 %collective-permute-start.1 = (bf16[4,2,256,128]{3,2,0,1:T(8,128)(2,1)}, bf16[4,2,256,128]{3,2,0,1:T(8,128)(2,1)}, u32[]{:S(2)}, u32[]{:S(2)}) collective-permute-start(bf16[4,2,256,128]{3,2,0,1:T(8,128)(2,1)} %get-tuple-element.6), channel_id=1, source_target_pairs={{0,2},{1,3},{2,0},{3,1},{4,6},{5,7},{6,4},{7,5},{8,10},{9,11},{10,... | collective-permute-start | bytes 1572872 | tf_op jit(solution)/shard_map/ppermute | solution.py:109
  31.8 24.2 %collective-permute-start.2 = (bf16[4,2,256,128]{3,2,0,1:T(8,128)(2,1)}, bf16[4,2,256,128]{3,2,0,1:T(8,128)(2,1)}, u32[]{:S(2)}, u32[]{:S(2)}) collective-permute-start(bf16[4,2,256,128]{3,2,0,1:T(8,128)(2,1)} %get-tuple-element.7), channel_id=1, source_target_pairs={{0,3},{1,2},{2,1},{3,0},{4,7},{5,6},{6,5},{7,4},{8,11},{9,10},{10,... | collective-permute-start | bytes 1572872 | tf_op jit(solution)/shard_map/ppermute | solution.py:109
  31.9 26.6 %collective-permute-start.3 = (bf16[4,2,256,128]{3,2,0,1:T(8,128)(2,1)}, bf16[4,2,256,128]{3,2,0,1:T(8,128)(2,1)}, u32[]{:S(2)}, u32[]{:S(2)}) collective-permute-start(bf16[4,2,256,128]{3,2,0,1:T(8,128)(2,1)} %get-tuple-element.8), channel_id=1, source_target_pairs={{0,4},{1,5},{2,6},{3,7},{4,0},{5,1},{6,2},{7,3},{8,12},{9,13},{10,... | collective-permute-start | bytes 1572872 | tf_op jit(solution)/shard_map/ppermute | solution.py:109
  35.7 6.6 %copy-start.4 = (bf16[4,2,256,128]{3,2,0,1:T(8,128)(2,1)S(1)}, bf16[4,2,256,128]{3,2,0,1:T(8,128)(2,1)}, u32[]{:S(2)}) copy-start(bf16[4,2,256,128]{3,2,0,1:T(8,128)(2,1)} %get-tuple-element.4) | copy-start | bytes 1572868
  35.8 8.0 %copy-start.7 = (bf16[4,2,256,128]{3,2,0,1:T(8,128)(2,1)S(1)}, bf16[4,2,256,128]{3,2,0,1:T(8,128)(2,1)}, u32[]{:S(2)}) copy-start(bf16[4,2,256,128]{3,2,0,1:T(8,128)(2,1)} %get-tuple-element.9) | copy-start | bytes 1572868
  35.8 12.8 %copy-start.5 = (bf16[4,2,256,128]{3,2,0,1:T(8,128)(2,1)S(1)}, bf16[4,2,256,128]{3,2,0,1:T(8,128)(2,1)}, u32[]{:S(2)}) copy-start(bf16[4,2,256,128]{3,2,0,1:T(8,128)(2,1)} %get-tuple-element.3) | copy-start | bytes 1572868
  35.8 43.9 %collective-permute-start.4 = (bf16[4,2,256,128]{3,2,0,1:T(8,128)(2,1)}, bf16[4,2,256,128]{3,2,0,1:T(8,128)(2,1)S(1)}, u32[]{:S(2)}, u32[]{:S(2)}) collective-permute-start(bf16[4,2,256,128]{3,2,0,1:T(8,128)(2,1)} %get-tuple-element.10), channel_id=1, source_target_pairs={{0,5},{1,4},{2,7},{3,6},{4,1},{5,0},{6,3},{7,2},{8,13},{9,12},{10,... | collective-permute-start | bytes 1572872 | tf_op jit(solution)/shard_map/ppermute | solution.py:109
  43.7 37.3 %collective-permute-start.5 = (bf16[4,2,256,128]{3,2,0,1:T(8,128)(2,1)S(1)}, bf16[4,2,256,128]{3,2,0,1:T(8,128)(2,1)S(1)}, u32[]{:S(2)}, u32[]{:S(2)}) collective-permute-start(bf16[4,2,256,128]{3,2,0,1:T(8,128)(2,1)S(1)} %copy-done.7), channel_id=1, source_target_pairs={{0,6},{1,7},{2,4},{3,5},{4,2},{5,3},{6,0},{7,1},{8,14},{9,15},{10,... | collective-permute-start | bytes 1572872 | tf_op jit(solution)/shard_map/ppermute | solution.py:109
  48.6 33.9 %collective-permute-start.6 = (bf16[4,2,256,128]{3,2,0,1:T(8,128)(2,1)S(1)}, bf16[4,2,256,128]{3,2,0,1:T(8,128)(2,1)S(1)}, u32[]{:S(2)}, u32[]{:S(2)}) collective-permute-start(bf16[4,2,256,128]{3,2,0,1:T(8,128)(2,1)S(1)} %copy-done.5), channel_id=1, source_target_pairs={{0,7},{1,6},{2,5},{3,4},{4,3},{5,2},{6,1},{7,0},{8,15},{9,14},{10,... | collective-permute-start | bytes 1572872 | tf_op jit(solution)/shard_map/ppermute | solution.py:109
  194.3 3.2 copy-start.1
  197.5 17.1 %copy-start.11 = (f32[128]{0:T(128)S(1)}, f32[128]{0:T(128)}, u32[]{:S(2)}) copy-start(f32[128]{0:T(128)} %param.11) | copy-start | bytes 1540
  361.7 12.5 %copy-start.10 = (f32[128]{0:T(128)}, f32[128]{0:T(128)S(1)}, u32[]{:S(2)}) copy-start(f32[128]{0:T(128)S(1)} %fusion.21) | copy-start | bytes 1540
Sparse Core Ops, SparseCore 0:
  214.8 119.0 all-reduce.1
